TPU v7x, 32 devices: a whole 2x2x4 slice. The times are simulated.
32 devices in a mesh: group: 2 (over x), lag: 16 (over z, y, core).
Axes of the slice: x: 2, y: 2, z: 4, core: 2. Of those that a mesh axis runs over, the one named last changes fastest.
Arguments:
- markov: bfloat16 [64, 32, 8192], P(('group', 'lag')), parts along dimension 0, may hold values from -40 to 40
- omega: int32 [512, 32], replicated, may hold values from -4 to 4
Outputs:
- basis_rows: float32 [64, 32, 8192], P(('group', 'lag')), parts along dimension 0
- coupled: float32 [64, 512], P('group'), parts along dimension 0
There are 2 independent parts, one for each index of `group`. A program takes and returns all parts, laid end to end along the dimension named above; an argument that names none is the same for every part. Nothing has to cross between parts.
All inputs are finite; a program needn't handle non-finite values.
Results may differ from a plain program's by a relative error of at most 0.0003.
Values may be sent and summed in bfloat16 or wider, within the bound.
A program may use at most 128 MiB of HBM per device.

v0:
```python
import math

import jax
import jax.numpy as jnp
from jax import lax
from jax.sharding import PartitionSpec as P

J = 16


def from_behind(value, axis, steps):
    count = lax.axis_size(axis)
    first, last = (max(0, -steps), min(count, count - steps))
    return lax.ppermute(value, axis, [(source, source + steps) for source in range(first, last)])


def test_matrix(omega):
    return (omega.astype(jnp.float32) * 0.25).astype(jnp.bfloat16)


def whiten(factor, sketch):
    count, rank_size, width = sketch.shape
    flattened = jnp.moveaxis(sketch, 1, 0).reshape(rank_size, count * width)
    solved = jax.scipy.linalg.solve_triangular(factor, flattened, lower=True)
    return jnp.moveaxis(solved.reshape(rank_size, count, width), 0, 1)


def finish(sketch, slab_at, total_rows):
    local_gram = jnp.einsum("krp,ksp->rs", sketch, sketch, precision=lax.Precision.HIGHEST)
    gram_matrix = lax.psum(local_gram, "lag") / total_rows
    factor = jnp.linalg.cholesky(gram_matrix)
    basis_local = whiten(factor, sketch)
    blocks = [
        jnp.einsum(
            "krp,kcp->rc",
            basis_local,
            slab_at(offset).astype(jnp.float32),
            precision=lax.Precision.HIGHEST,
        )
        for offset in range(J)
    ]
    coupled = lax.psum(jnp.concatenate(blocks, axis=1), "lag") / math.sqrt(total_rows)
    return (basis_local, coupled)


def per_device(markov, omega):
    lag_count, inputs, rows = markov.shape
    lags_total = lag_count * lax.axis_size("lag")
    total_rows = lags_total * rows
    probes = test_matrix(omega)
    reach = (J + lag_count - 2) // lag_count
    pieces = [markov]
    carried = markov
    for passage in range(reach):
        carried = from_behind(carried, "lag", -1)
        pieces.append(carried)
    extended = jnp.concatenate(pieces, axis=0)
    sketch = jnp.stack(
        [
            lax.dot_general(
                probes,
                extended[first : first + J].reshape(J * inputs, rows),
                (((0,), (0,)), ((), ())),
                preferred_element_type=jnp.float32,
            )
            for first in range(lag_count)
        ]
    )
    basis_rows, coupled = finish(
        sketch, lambda offset: extended[offset : offset + lag_count], total_rows
    )
    return (basis_rows, coupled)


def solution(mesh):
    return jax.shard_map(
        per_device,
        mesh=mesh,
        in_specs=(P(("group", "lag"), None, None), P()),
        out_specs=(P(("group", "lag"), None, None), P("group", None)),
        check_vma=False,
    )
```

profile of v0, /device:TPU:0, one launch (start us, length us, event | category | flops | bytes accessed | tf_op | source)
XLA Modules:
  0.0 337.9 jit_solution(12788695914915859837)
XLA Ops:
  7.2 1.3 collective-permute-start
  8.5 3.5 %collective-permute-done = bf16[2,32,8192]{2,1,0:T(8,128)(2,1)S(1)} collective-permute-done((bf16[2,32,8192]{2,1,0:T(8,128)(2,1)}, bf16[2,32,8192]{2,1,0:T(8,128)(2,1)S(1)}, u32[]{:S(2)}, u32[]{:S(2)}) %collective-permute-start) | collective-permute-done | bytes 1048608 | tf_op jit(solution)/shard_map/ppermute | solution.py:14
  12.0 1.3 collective-permute-start.1
  13.3 15.7 %collective-permute-done.1 = bf16[2,32,8192]{2,1,0:T(8,128)(2,1)S(1)} collective-permute-done((bf16[2,32,8192]{2,1,0:T(8,128)(2,1)S(1)}, bf16[2,32,8192]{2,1,0:T(8,128)(2,1)S(1)}, u32[]{:S(2)}, u32[]{:S(2)}) %collective-permute-start.1) | collective-permute-done | bytes 1048608 | tf_op jit(solution)/shard_map/ppermute | solution.py:14
  28.9 1.3 collective-permute-start.2
  30.2 14.8 %collective-permute-done.2 = bf16[2,32,8192]{2,1,0:T(8,128)(2,1)S(1)} collective-permute-done((bf16[2,32,8192]{2,1,0:T(8,128)(2,1)S(1)}, bf16[2,32,8192]{2,1,0:T(8,128)(2,1)S(1)}, u32[]{:S(2)}, u32[]{:S(2)}) %collective-permute-start.2) | collective-permute-done | bytes 1048608 | tf_op jit(solution)/shard_map/ppermute | solution.py:14
  45.0 1.3 collective-permute-start.3
  46.3 2.3 constant_dynamic-update-slice_fusion.7
  48.7 12.5 %collective-permute-done.3 = bf16[2,32,8192]{2,1,0:T(8,128)(2,1)S(1)} collective-permute-done((bf16[2,32,8192]{2,1,0:T(8,128)(2,1)S(1)}, bf16[2,32,8192]{2,1,0:T(8,128)(2,1)S(1)}, u32[]{:S(2)}, u32[]{:S(2)}) %collective-permute-start.3) | collective-permute-done | bytes 1048608 | tf_op jit(solution)/shard_map/ppermute | solution.py:14
  61.1 1.3 collective-permute-start.4
  62.4 1.1 constant_dynamic-update-slice_fusion.6
  63.6 1.1 constant_dynamic-update-slice_fusion.5
  64.7 12.6 %collective-permute-done.4 = bf16[2,32,8192]{2,1,0:T(8,128)(2,1)S(1)} collective-permute-done((bf16[2,32,8192]{2,1,0:T(8,128)(2,1)S(1)}, bf16[2,32,8192]{2,1,0:T(8,128)(2,1)S(1)}, u32[]{:S(2)}, u32[]{:S(2)}) %collective-permute-start.4) | collective-permute-done | bytes 1048608 | tf_op jit(solution)/shard_map/ppermute | solution.py:14
  77.3 1.3 collective-permute-start.5
  78.5 1.1 constant_dynamic-update-slice_fusion.4
  79.7 1.1 constant_dynamic-update-slice_fusion.3
  80.8 12.6 %collective-permute-done.5 = bf16[2,32,8192]{2,1,0:T(8,128)(2,1)S(1)} collective-permute-done((bf16[2,32,8192]{2,1,0:T(8,128)(2,1)S(1)}, bf16[2,32,8192]{2,1,0:T(8,128)(2,1)S(1)}, u32[]{:S(2)}, u32[]{:S(2)}) %collective-permute-start.5) | collective-permute-done | bytes 1048608 | tf_op jit(solution)/shard_map/ppermute | solution.py:14
  93.4 1.3 collective-permute-start.6
  94.7 1.1 constant_dynamic-update-slice_fusion.2
  95.8 1.1 constant_dynamic-update-slice_fusion.1
  96.9 12.6 %collective-permute-done.6 = bf16[2,32,8192]{2,1,0:T(8,128)(2,1)S(1)} collective-permute-done((bf16[2,32,8192]{2,1,0:T(8,128)(2,1)S(1)}, bf16[2,32,8192]{2,1,0:T(8,128)(2,1)S(1)}, u32[]{:S(2)}, u32[]{:S(2)}) %collective-permute-start.6) | collective-permute-done | bytes 1048608 | tf_op jit(solution)/shard_map/ppermute | solution.py:14
  109.5 1.3 collective-permute-start.7
  110.8 1.2 constant_dynamic-update-slice_fusion
  112.0 1.5 convolution_bitcast_fusion.2
  113.5 12.1 %collective-permute-done.7 = bf16[2,32,8192]{2,1,0:T(8,128)(2,1)S(1)} collective-permute-done((bf16[2,32,8192]{2,1,0:T(8,128)(2,1)S(1)}, bf16[2,32,8192]{2,1,0:T(8,128)(2,1)S(1)}, u32[]{:S(2)}, u32[]{:S(2)}) %collective-permute-start.7) | collective-permute-done | bytes 1048608 | tf_op jit(solution)/shard_map/ppermute | solution.py:14
  125.6 1.2 constant_dynamic-update-slice_fusion.8
  126.8 7.7 %slice.58 = bf16[16,32,8192]{2,1,0:T(8,128)(2,1)} slice(bf16[18,32,8192]{2,1,0:T(8,128)(2,1)} %constant_dynamic-update-slice_fusion.8), slice={[1:17], [0:32], [0:8192]} | slice | bytes 16777216 | tf_op jit(solution)/shard_map/slice | solution.py:62
  134.5 5.9 %convolution_bitcast_fusion.1 = f32[1,32,8192]{2,1,0:T(8,128)} fusion(bf16[512,8192]{1,0:T(8,128)(2,1)} %bitcast.95, s32[512,32]{0,1:T(8,128)S(1)} %copy-done.13), kind=kOutput, calls=%fused_computation.1 | convolution fusion | flops 268484608 | bytes 9502720 | tf_op jit(solution)/shard_map/dot_general | solution.py:60
  140.4 3.3 fusion.4
  143.7 73.3 %psum.14 = f32[32,32]{0,1:T(8,128)S(1)} all-reduce(f32[32,32]{0,1:T(8,128)S(1)} %fusion.4), channel_id=1, replica_groups=mesh['group'=2,'lag'=16] {'lag'}, use_global_device_ids=true, to_apply=%region_0.0 | all-reduce | flops 1024 | bytes 8192 | tf_op jit(solution)/shard_map/psum | solution.py:30
  217.1 2.9 cholesky.16
  221.3 2.4 custom-call.7
  223.8 3.5 %convolution_bitcast_fusion = f32[2,32,8192]{2,1,0:T(8,128)S(1)} fusion(f32[1,32,32]{1,2,0:T(8,128)S(1)} %custom-call.7, f32[1,32,8192]{2,1,0:T(8,128)} %convolution_bitcast_fusion.1, f32[1,32,8192]{2,1,0:T(8,128)} %copy-done.10), kind=kOutput, calls=%fused_computation | convolution fusion | flops 201850880 | bytes 4198400 | tf_op jit(solution)/shard_map/jit(_solve_triangular)/triangular_solve | solution.py:24
  229.6 1.1 convolution_bitcast_fusion.3
  232.0 1.1 convolution_bitcast_fusion.5
  234.3 1.1 convolution_bitcast_fusion.7
  235.5 1.1 convolution_bitcast_fusion.8
  236.7 1.1 convolution_bitcast_fusion.9
  237.8 1.2 convolution_bitcast_fusion.10
  239.0 1.1 convolution_bitcast_fusion.11
  240.1 1.1 convolution_bitcast_fusion.12
  241.3 1.1 convolution_bitcast_fusion.13
  242.4 1.1 convolution_bitcast_fusion.14
  243.5 1.1 convolution_bitcast_fusion.15
  244.7 1.1 convolution_bitcast_fusion.16
  245.8 1.1 convolution_bitcast_fusion.17
  247.7 81.8 %all-reduce.2.cloned.1.call-done = f32[32,512]{1,0:T(8,128)} async-done(((f32[32,512]{1,0:T(8,128)}), f32[32,512]{1,0:T(8,128)}) %all-reduce.2.cloned.1.call-update) | async-done | bytes 65552 | tf_op jit(solution)/shard_map/psum | solution.py:42
  329.6 1.5 broadcast_multiply_fusion
  (40 shorter events, 7.1 us)
Async XLA Ops:
  7.2 322.4 %all-reduce.2.cloned.1.call-start = ((), (), s32[]{:S(2)}) async-start(), calls=%async_computation | async-start | bytes 131072 | tf_op jit(solution)/shard_map/psum | solution.py:42
  7.2 4.8 %collective-permute-start = (bf16[2,32,8192]{2,1,0:T(8,128)(2,1)}, bf16[2,32,8192]{2,1,0:T(8,128)(2,1)S(1)}, u32[]{:S(2)}, u32[]{:S(2)}) collective-permute-start(bf16[2,32,8192]{2,1,0:T(8,128)(2,1)} %param.2), channel_id=1, source_target_pairs={{1,0},{2,1},{3,2},{4,3},{5,4},{6,5},{7,6},{8,7},{9,8},{10,9},{11,1... | collective-permute-start | bytes 3145736 | tf_op jit(solution)/shard_map/ppermute | solution.py:14
  12.0 17.0 %collective-permute-start.1 = (bf16[2,32,8192]{2,1,0:T(8,128)(2,1)S(1)}, bf16[2,32,8192]{2,1,0:T(8,128)(2,1)S(1)}, u32[]{:S(2)}, u32[]{:S(2)}) collective-permute-start(bf16[2,32,8192]{2,1,0:T(8,128)(2,1)S(1)} %collective-permute-done), channel_id=1, source_target_pairs={{1,0},{2,1},{3,2},{4,3},{5,4},{6,5},{7,6},{8,7},{9,8},{10,9},{11,1... | collective-permute-start | bytes 3145736 | tf_op jit(solution)/shard_map/ppermute | solution.py:14
  28.9 16.1 %collective-permute-start.2 = (bf16[2,32,8192]{2,1,0:T(8,128)(2,1)S(1)}, bf16[2,32,8192]{2,1,0:T(8,128)(2,1)S(1)}, u32[]{:S(2)}, u32[]{:S(2)}) collective-permute-start(bf16[2,32,8192]{2,1,0:T(8,128)(2,1)S(1)} %collective-permute-done.1), channel_id=1, source_target_pairs={{1,0},{2,1},{3,2},{4,3},{5,4},{6,5},{7,6},{8,7},{9,8},{10,9},{11,1... | collective-permute-start | bytes 3145736 | tf_op jit(solution)/shard_map/ppermute | solution.py:14
  45.0 16.1 %collective-permute-start.3 = (bf16[2,32,8192]{2,1,0:T(8,128)(2,1)S(1)}, bf16[2,32,8192]{2,1,0:T(8,128)(2,1)S(1)}, u32[]{:S(2)}, u32[]{:S(2)}) collective-permute-start(bf16[2,32,8192]{2,1,0:T(8,128)(2,1)S(1)} %collective-permute-done.2), channel_id=1, source_target_pairs={{1,0},{2,1},{3,2},{4,3},{5,4},{6,5},{7,6},{8,7},{9,8},{10,9},{11,1... | collective-permute-start | bytes 3145736 | tf_op jit(solution)/shard_map/ppermute | solution.py:14
  61.1 18.5 %copy-start.1 = (bf16[2,32,8192]{2,1,0:T(8,128)(2,1)}, bf16[2,32,8192]{2,1,0:T(8,128)(2,1)S(1)}, u32[]{:S(2)}) copy-start(bf16[2,32,8192]{2,1,0:T(8,128)(2,1)S(1)} %collective-permute-done.3) | copy-start | bytes 3145732
  61.1 16.1 %collective-permute-start.4 = (bf16[2,32,8192]{2,1,0:T(8,128)(2,1)S(1)}, bf16[2,32,8192]{2,1,0:T(8,128)(2,1)S(1)}, u32[]{:S(2)}, u32[]{:S(2)}) collective-permute-start(bf16[2,32,8192]{2,1,0:T(8,128)(2,1)S(1)} %collective-permute-done.3), channel_id=1, source_target_pairs={{1,0},{2,1},{3,2},{4,3},{5,4},{6,5},{7,6},{8,7},{9,8},{10,9},{11,1... | collective-permute-start | bytes 3145736 | tf_op jit(solution)/shard_map/ppermute | solution.py:14
  77.3 17.4 %copy-start.3 = (bf16[2,32,8192]{2,1,0:T(8,128)(2,1)}, bf16[2,32,8192]{2,1,0:T(8,128)(2,1)S(1)}, u32[]{:S(2)}) copy-start(bf16[2,32,8192]{2,1,0:T(8,128)(2,1)S(1)} %collective-permute-done.4) | copy-start | bytes 3145732
  77.3 16.1 %collective-permute-start.5 = (bf16[2,32,8192]{2,1,0:T(8,128)(2,1)S(1)}, bf16[2,32,8192]{2,1,0:T(8,128)(2,1)S(1)}, u32[]{:S(2)}, u32[]{:S(2)}) collective-permute-start(bf16[2,32,8192]{2,1,0:T(8,128)(2,1)S(1)} %collective-permute-done.4), channel_id=1, source_target_pairs={{1,0},{2,1},{3,2},{4,3},{5,4},{6,5},{7,6},{8,7},{9,8},{10,9},{11,1... | collective-permute-start | bytes 3145736 | tf_op jit(solution)/shard_map/ppermute | solution.py:14
  93.4 3.5 %copy-start.5 = (bf16[2,32,8192]{2,1,0:T(8,128)(2,1)}, bf16[2,32,8192]{2,1,0:T(8,128)(2,1)S(1)}, u32[]{:S(2)}) copy-start(bf16[2,32,8192]{2,1,0:T(8,128)(2,1)S(1)} %collective-permute-done.5) | copy-start | bytes 3145732
  93.4 16.1 %collective-permute-start.6 = (bf16[2,32,8192]{2,1,0:T(8,128)(2,1)S(1)}, bf16[2,32,8192]{2,1,0:T(8,128)(2,1)S(1)}, u32[]{:S(2)}, u32[]{:S(2)}) collective-permute-start(bf16[2,32,8192]{2,1,0:T(8,128)(2,1)S(1)} %collective-permute-done.5), channel_id=1, source_target_pairs={{1,0},{2,1},{3,2},{4,3},{5,4},{6,5},{7,6},{8,7},{9,8},{10,9},{11,1... | collective-permute-start | bytes 3145736 | tf_op jit(solution)/shard_map/ppermute | solution.py:14
  96.9 15.1 %copy-start.13 = (s32[512,32]{0,1:T(8,128)S(1)}, s32[512,32]{0,1:T(8,128)}, u32[]{:S(2)}) copy-start(s32[512,32]{0,1:T(8,128)} %param.3) | copy-start | bytes 196612
  109.5 4.0 %copy-start.7 = (bf16[2,32,8192]{2,1,0:T(8,128)(2,1)}, bf16[2,32,8192]{2,1,0:T(8,128)(2,1)S(1)}, u32[]{:S(2)}) copy-start(bf16[2,32,8192]{2,1,0:T(8,128)(2,1)S(1)} %collective-permute-done.6) | copy-start | bytes 3145732
  109.5 16.1 %collective-permute-start.7 = (bf16[2,32,8192]{2,1,0:T(8,128)(2,1)S(1)}, bf16[2,32,8192]{2,1,0:T(8,128)(2,1)S(1)}, u32[]{:S(2)}, u32[]{:S(2)}) collective-permute-start(bf16[2,32,8192]{2,1,0:T(8,128)(2,1)S(1)} %collective-permute-done.6), channel_id=1, source_target_pairs={{1,0},{2,1},{3,2},{4,3},{5,4},{6,5},{7,6},{8,7},{9,8},{10,9},{11,1... | collective-permute-start | bytes 3145736 | tf_op jit(solution)/shard_map/ppermute | solution.py:14
  113.5 26.9 %copy-start.10 = (f32[1,32,8192]{2,1,0:T(8,128)}, f32[1,32,8192]{2,1,0:T(8,128)S(1)}, u32[]{:S(2)}) copy-start(f32[1,32,8192]{2,1,0:T(8,128)S(1)} %convolution_bitcast_fusion.2) | copy-start | bytes 3145732
  125.6 8.9 %copy-start.11 = (bf16[2,32,8192]{2,1,0:T(8,128)(2,1)}, bf16[2,32,8192]{2,1,0:T(8,128)(2,1)S(1)}, u32[]{:S(2)}) copy-start(bf16[2,32,8192]{2,1,0:T(8,128)(2,1)S(1)} %collective-permute-done.7) | copy-start | bytes 3145732
  223.8 3.5 %copy-start.9 = (bf16[2,32,8192]{2,1,0:T(8,128)(2,1)S(1)}, bf16[2,32,8192]{2,1,0:T(8,128)(2,1)}, u32[]{:S(2)}) copy-start(bf16[2,32,8192]{2,1,0:T(8,128)(2,1)} %param.2) | copy-start | bytes 3145732
  227.3 18.5 %copy-start = (f32[2,32,8192]{2,1,0:T(8,128)}, f32[2,32,8192]{2,1,0:T(8,128)S(1)}, u32[]{:S(2)}) copy-start(f32[2,32,8192]{2,1,0:T(8,128)S(1)} %convolution_bitcast_fusion) | copy-start | bytes 6291460
  227.3 2.0 copy-start.8
  227.4 2.3 copy-start.12
  230.8 1.2 copy-start.6
  233.1 1.2 copy-start.4
  235.4 1.2 copy-start.2
Sparse Core Ops, SparseCore 0:
  247.8 81.6 all-reduce.1
where the time goes:
time: 340 us; the launch traced here: 338 us
  waiting for transfers between devices  178 us (52%)
  blocking collectives  73.3 us (22%)
  matrix products  32.2 us (9%)
  local copies, waits for them, and re-layouts  21.5 us (6%)
  between operations  14.3 us (4%)
  starting transfers between devices  10.3 us (3%)
  other arithmetic  8.17 us (2%)
    ppermute x8, waiting for transfers between devices, from_behind(): lax.ppermute(value, axis, [(source, source + steps) for source in range(f...  96.2 us
    psum x1, waiting for transfers between devices, finish(): lax.psum(jnp.concatenate(blocks, axis=1), 'lag') / math.sqrt(total_rows)  81.8 us
    psum x1, blocking collectives, finish(): gram_matrix = lax.psum(local_gram, 'lag') / total_rows  73.3 us
    dot_general x16, matrix products, finish(): jnp.einsum('krp,kcp->rc', basis_local, slab_at(offset).astype(jnp.float32...  17.9 us
    unnamed x35, local copies, waits for them, and re-layouts  10.6 us
    ppermute x8, starting transfers between devices, from_behind(): lax.ppermute(value, axis, [(source, source + steps) for source in range(f...  10.3 us
    slice x1, local copies, waits for them, and re-layouts, per_device(): extended[first:first + J].reshape(J * inputs, rows)  7.69 us
    dot_general x2, matrix products, per_device(): lax.dot_general(probes, extended[first:first + J].reshape(J * inputs, row...  7.44 us
  transfers between devices with their start and end apart: 9, of which 9 were waited for; matrix products, arithmetic and copies ran while one was open for 3% of the time, Pallas kernels for 0%

commit v1 on v0

v1 whole, which is shorter than its diff:
```python
import functools
import math

import jax
import jax.numpy as jnp
from jax import lax
from jax.experimental import pallas as pl
from jax.experimental.pallas import tpu as pltpu
from jax.sharding import PartitionSpec as P

J = 16
TEAM = 4
CHUNKS = 4
HIGH = lax.Precision.HIGHEST
NT = (((1,), (1,)), ((), ()))


def split3(value):
    high = value.astype(jnp.bfloat16)
    rest = value - high.astype(jnp.float32)
    middle = rest.astype(jnp.bfloat16)
    low = (rest - middle.astype(jnp.float32)).astype(jnp.bfloat16)
    return high, middle, low


def inverse_factor(gram):
    size = gram.shape[0]
    rows = lax.broadcasted_iota(jnp.int32, (size, 128), 0)
    lanes = lax.broadcasted_iota(jnp.int32, (size, 128), 1)
    work = gram + jnp.where(lanes == rows + size, 1.0, 0.0)
    for step in range(size):
        pivot_row = work[step : step + 1, :]
        pivot = pivot_row[:, step : step + 1]
        scale = lax.rsqrt(pivot)
        scale = scale * (1.5 - 0.5 * pivot * scale * scale)
        unit_row = pivot_row * scale
        column = work[:, step : step + 1] * scale
        work = jnp.where(
            rows > step, work - column * unit_row, jnp.where(rows == step, unit_row, work)
        )
    return pltpu.roll(work, 128 - size, 1)[:, :size]


def kernel(count, x_ref, omega_ref, basis_ref, coupled_ref, halo, weights, sk, own, corr, gram_acc,
           msg, rbuf, kred, kfin, p1s, p1r, dns, dnr, fws, fwr, srs, srr, m1s, m1r, m2s, m2r):
    per, inputs, width = x_ref.shape
    rank = omega_ref.shape[1]
    quarter = width // TEAM
    piece = quarter // CHUNKS
    level_lags = per * TEAM
    reach = J - 1
    lags = halo.shape[1]
    levels = count // TEAM
    total_rows = count * per * width
    me = lax.axis_index("lag")
    level, place = me // TEAM, me % TEAM
    mates = [place, place + 1 - 2 * (place % 2), (place + 2) % TEAM, TEAM - 1 - place]
    below = lax.rem(me + count - TEAM, count)

    barrier = pltpu.get_barrier_semaphore()

    @pl.loop(1, count)
    def _(step):
        pl.semaphore_signal(barrier, inc=1, device_id={"lag": lax.rem(me + step, count)},
                            device_id_type=pl.DeviceIdType.MESH)

    pl.semaphore_wait(barrier, count - 1)

    def remote(src, dst, send, recv, target):
        return pltpu.make_async_remote_copy(
            src_ref=src, dst_ref=dst, send_sem=send, recv_sem=recv,
            device_id={"lag": target}, device_id_type=pl.DeviceIdType.MESH)

    def columns(who, k):
        return pl.ds(pl.multiple_of(who * quarter + k * piece, 128), piece)

    def spread(k, s):
        mate = mates[s]
        return remote(x_ref.at[:, :, columns(mate, k)], halo.at[k, pl.ds(per * place, per)],
                      p1s.at[k, s], p1r.at[k, place], level * TEAM + mate)

    def spread_in(k, s):
        mate = mates[s]
        dst = halo.at[k, pl.ds(per * mate, per)]
        return remote(dst, dst, p1s.at[k, s], p1r.at[k, mate], level * TEAM + mate)

    def down(k, s):
        mate = mates[s]
        src = x_ref.at[:, :, columns(place, k)] if s == 0 else halo.at[k, pl.ds(per * mate, per)]
        return remote(src, halo.at[k, pl.ds(level_lags + per * mate, per)],
                      dns.at[k, s], dnr.at[k, mate], below)

    def forward(k):
        return remote(halo.at[k, pl.ds(level_lags, reach - level_lags)],
                      halo.at[k, pl.ds(2 * level_lags, reach - level_lags)],
                      fws.at[k], fwr.at[k], below)

    def give_back(k, s):
        mate = mates[s]
        return remote(sk.at[k, pl.ds(per * mate, per)], own.at[place, k],
                      srs.at[k, s], srr.at[k, place], level * TEAM + mate)

    def give_back_in(k, s):
        mate = mates[s]
        return remote(own.at[mate, k], own.at[mate, k], srs.at[k, s], srr.at[k, mate],
                      level * TEAM + mate)

    for k in range(CHUNKS):
        for s in (2, 3, 1):
            spread(k, s).start()

    @pl.when(level > 0)
    def _():
        down(0, 0).start()

    for k in range(CHUNKS):
        halo[k, pl.ds(per * place, per)] = x_ref[:, :, columns(place, k)]
        halo[k, lags - 1] = jnp.zeros((inputs, piece), jnp.bfloat16)

    @pl.when(level >= levels - 2)
    def _():
        for k in range(CHUNKS):
            halo[k, 2 * level_lags : lags - 1] = jnp.zeros(
                (lags - 1 - 2 * level_lags, inputs, piece), jnp.bfloat16)

    @pl.when(level == levels - 1)
    def _():
        for k in range(CHUNKS):
            halo[k, level_lags : 2 * level_lags] = jnp.zeros(
                (level_lags, inputs, piece), jnp.bfloat16)

    def own_down(k):
        for s in range(TEAM):
            if s:
                spread_in(k, s).wait_recv()
            if s or k:
                @pl.when(level > 0)
                def _():
                    down(k, s).start()

    def pass_on(k):
        @pl.when(level < levels - 1)
        def _():
            for s in range(TEAM):
                down(k, s).wait_recv()

            @pl.when(level > 0)
            def _():
                forward(k).start()

    def compute(k):
        @pl.when(level < levels - 2)
        def _():
            forward(k).wait_recv()

        window = halo[k].reshape(lags * inputs, piece)
        sketch = jnp.dot(weights[...], window, preferred_element_type=jnp.float32)
        sk[k] = sketch.reshape(level_lags, rank, piece)
        for s in (2, 3, 1):
            give_back(k, s).start()
        own[place, k] = sk[k, pl.ds(per * place, per)]
        parts = split3(sketch)
        product = sum(
            lax.dot_general(part, window, NT, preferred_element_type=jnp.float32)
            for part in reversed(parts)
        )
        corr[...] = product if k == 0 else corr[...] + product
        wide = jnp.concatenate([sketch[i * rank : (i + 1) * rank] for i in range(level_lags)], axis=1)
        local = lax.dot_general(wide, wide, NT, precision=HIGH, preferred_element_type=jnp.float32)
        gram_acc[:, :rank] = local if k == 0 else gram_acc[:, :rank] + local

    own_down(0)
    own_down(1)
    gram_acc[...] = jnp.zeros_like(gram_acc)
    probes = omega_ref[...].astype(jnp.float32) * 0.25
    identity = jnp.where(
        lax.broadcasted_iota(jnp.int32, (rank, rank), 0)
        == lax.broadcasted_iota(jnp.int32, (rank, rank), 1), 1.0, 0.0)
    turned = lax.dot_general(identity, probes, NT, preferred_element_type=jnp.float32)
    band = jnp.concatenate(
        [turned, jnp.zeros((rank, weights.shape[1] - turned.shape[1]), jnp.float32)], axis=1)
    for i in range(level_lags):
        row = band if i == 0 else pltpu.roll(band, i * inputs, 1)
        weights[i * rank : (i + 1) * rank, :] = row.astype(jnp.bfloat16)
    pass_on(0)
    for k in range(2, CHUNKS):
        own_down(k)
        pass_on(k - 1)
        if k > 2:
            compute(k - 3)
    compute(CHUNKS - 3)
    pass_on(CHUNKS - 1)
    compute(CHUNKS - 2)
    compute(CHUNKS - 1)

    folded = corr[0:rank, : J * inputs]
    for i in range(1, level_lags):
        turned_back = pltpu.roll(corr[i * rank : (i + 1) * rank, :], lags * inputs - i * inputs, 1)
        folded = folded + turned_back[:, : J * inputs]
    packed = gram_acc[0:8, :]
    for b in range(1, rank // 8):
        packed = packed + pltpu.roll(gram_acc[8 * b : 8 * b + 8, :], b * rank, 1)
    tiles_across = J * inputs // 128
    tiles = (rank // 8) * tiles_across
    for d in range(count):
        msg[d, 0] = packed
        if d < tiles:
            a, b = divmod(d, tiles_across)
            msg[d, 1] = folded[8 * a : 8 * a + 8, 128 * b : 128 * b + 128]
        else:
            msg[d, 1] = jnp.zeros((8, 128), jnp.float32)

    def partial(step):
        other = lax.rem(me + step, count)
        return remote(msg.at[other], rbuf.at[me], m1s.at[step], m1r.at[me], other)

    def partial_in(step):
        other = lax.rem(me + step, count)
        return remote(msg.at[other], rbuf.at[other], m1s.at[step], m1r.at[other], other)

    def whole(step):
        other = lax.rem(me + step, count)
        return remote(kred, kfin.at[me], m2s.at[step], m2r.at[me], other)

    def whole_in(step):
        other = lax.rem(me + step, count)
        return remote(kred, kfin.at[other], m2s.at[step], m2r.at[other], other)

    @pl.loop(1, count)
    def _(step):
        partial(step).start()

    rbuf[me] = msg[me]

    @pl.loop(1, count)
    def _(step):
        partial_in(step).wait_recv()

    total = rbuf[0]
    for d in range(1, count):
        total = total + rbuf[d]
    kred[...] = total[1]
    kfin[me] = total[1]

    @pl.loop(1, count)
    def _(step):
        whole(step).start()

    lanes = lax.broadcasted_iota(jnp.int32, (8, 128), 1)
    blocks = []
    for b in range(rank // 8):
        block = total[0] if b == 0 else pltpu.roll(total[0], 128 - b * rank, 1)
        blocks.append(jnp.where(lanes < rank, block, 0.0))
    inverse = inverse_factor(jnp.concatenate(blocks, axis=0) * (1.0 / total_rows))

    for k in range(CHUNKS):
        for s in range(1, TEAM):
            give_back_in(k, s).wait_recv()
    for q in range(TEAM):
        for k in range(CHUNKS):
            for g in range(per):
                basis_ref[g, :, q * quarter + k * piece : q * quarter + (k + 1) * piece] = jnp.dot(
                    inverse, own[q, k, g], precision=HIGH, preferred_element_type=jnp.float32)

    @pl.loop(1, count)
    def _(step):
        whole_in(step).wait_recv()

    summed = jnp.concatenate(
        [jnp.concatenate([kfin[a * tiles_across + b] for b in range(tiles_across)], axis=1)
         for a in range(rank // 8)], axis=0)
    coupled_ref[...] = jnp.dot(
        inverse, summed, precision=HIGH, preferred_element_type=jnp.float32
    ) * (1.0 / math.sqrt(total_rows))

    for k in range(CHUNKS):
        for s in range(1, TEAM):
            spread(k, s).wait_send()
            give_back(k, s).wait_send()

    @pl.when(level > 0)
    def _():
        for k in range(CHUNKS):
            for s in range(TEAM):
                down(k, s).wait_send()

    @pl.when(jnp.logical_and(level > 0, level < levels - 1))
    def _():
        for k in range(CHUNKS):
            forward(k).wait_send()

    @pl.loop(1, count)
    def _(step):
        partial(step).wait_send()
        whole(step).wait_send()


def per_device(count, markov, omega):
    per, inputs, width = markov.shape
    rank = omega.shape[1]
    piece = width // TEAM // CHUNKS
    level_lags = per * TEAM
    lags = level_lags + J
    dma = pltpu.SemaphoreType.DMA
    vmem = pl.BlockSpec(memory_space=pltpu.VMEM)
    return pl.pallas_call(
        functools.partial(kernel, count),
        out_shape=(
            jax.ShapeDtypeStruct((per, rank, width), jnp.float32),
            jax.ShapeDtypeStruct((rank, J * inputs), jnp.float32),
        ),
        in_specs=[vmem, vmem],
        out_specs=(vmem, vmem),
        scratch_shapes=[
            pltpu.VMEM((CHUNKS, lags, inputs, piece), jnp.bfloat16),
            pltpu.VMEM((level_lags * rank, lags * inputs), jnp.bfloat16),
            pltpu.VMEM((CHUNKS, level_lags, rank, piece), jnp.float32),
            pltpu.VMEM((TEAM, CHUNKS, per, rank, piece), jnp.float32),
            pltpu.VMEM((level_lags * rank, lags * inputs), jnp.float32),
            pltpu.VMEM((rank, 128), jnp.float32),
            pltpu.VMEM((count, 2, 8, 128), jnp.float32),
            pltpu.VMEM((count, 2, 8, 128), jnp.float32),
            pltpu.VMEM((8, 128), jnp.float32),
            pltpu.VMEM((count, 8, 128), jnp.float32),
            dma((CHUNKS, TEAM)), dma((CHUNKS, TEAM)), dma((CHUNKS, TEAM)), dma((CHUNKS, TEAM)),
            dma((CHUNKS,)), dma((CHUNKS,)), dma((CHUNKS, TEAM)), dma((CHUNKS, TEAM)),
            dma((count,)), dma((count,)), dma((count,)), dma((count,)),
        ],
        compiler_params=pltpu.CompilerParams(
            collective_id=0, has_side_effects=True, vmem_limit_bytes=40 * 2**20
        ),
        cost_estimate=pl.CostEstimate(flops=6 * 10**9, bytes_accessed=8 * 2**20, transcendentals=0),
    )(markov, omega)


def solution(mesh):
    return jax.shard_map(
        functools.partial(per_device, mesh.shape["lag"]),
        mesh=mesh,
        in_specs=(P(("group", "lag"), None, None), P()),
        out_specs=(P(("group", "lag"), None, None), P("group", None)),
        check_vma=False,
    )
```

time: 340 us -> 74 us (0.22)
  waiting for transfers between devices: 178 us -> 0 us
  blocking collectives: 73.3 us -> 0 us
  Pallas kernels: 0 us -> 69 us
  matrix products: 32.2 us -> 0 us
  local copies, waits for them, and re-layouts: 21.5 us -> 4.13 us
  between operations: 14.3 us -> 0.65 us
  starting transfers between devices: 10.3 us -> 0 us
  other arithmetic: 8.17 us -> 0 us
    ppermute x8 -> x0, waiting for transfers between devices: 96.2 us -> none  [from_behind(): lax.ppermute(value, axis, [(source, source + steps) for source in range(f...]
    psum x1 -> x0, waiting for transfers between devices: 81.8 us -> none  [finish(): lax.psum(jnp.concatenate(blocks, axis=1), 'lag') / math.sqrt(total_rows)]
    psum x1 -> x0, blocking collectives: 73.3 us -> none  [finish(): gram_matrix = lax.psum(local_gram, 'lag') / total_rows]
    pallas_call x0 -> x1, Pallas kernels: none -> 69 us  [per_device(): pl.pallas_call(functools.partial(kernel, count), out_shape=(jax.ShapeDtyp...]
    dot_general x19 -> x0, matrix products: 28.7 us -> none  [the longest x16 17.9 us: finish(): jnp.einsum('krp,kcp->rc', basis_local, slab_at(offset).astype(jnp.float32...]
    ppermute x8 -> x0, starting transfers between devices: 10.3 us -> none  [from_behind(): lax.ppermute(value, axis, [(source, source + steps) for source in range(f...]
    slice x1 -> x0, local copies, waits for them, and re-layouts: 7.69 us -> none  [per_device(): extended[first:first + J].reshape(J * inputs, rows)]
    another operation x5 -> x0, other arithmetic: 6.68 us -> none  [the longest x3 3.59 us: finish(): factor = jnp.linalg.cholesky(gram_matrix)]
  transfers between devices with their start and end apart: 9 -> 0, of which waited for: 9 -> 0; matrix products, arithmetic and copies ran while one was open for 3% -> 0% of each run, Pallas kernels for 0% -> 0%
where the time goes in v1:
time: 74 us; the launch traced here: 73.8 us
  Pallas kernels  69 us (93%)
  local copies, waits for them, and re-layouts  4.13 us (6%)
    pallas_call x1, Pallas kernels, per_device(): pl.pallas_call(functools.partial(kernel, count), out_shape=(jax.ShapeDtyp...  69 us
    unnamed x5, local copies, waits for them, and re-layouts  4.13 us

profile of v1, /device:TPU:0, one launch (start us, length us, event | category | flops | bytes accessed | tf_op | source)
XLA Modules:
  0.0 73.8 jit_solution(16352817401492722220)
XLA Ops:
  0.6 1.0 %copy.4.omega_ref = s32[512,32]{1,0:T(8,128)S(1)} copy(s32[512,32]{0,1:T(8,128)} %param.3) | data formatting | bytes 131072 | tf_op args[1]
  1.6 0.0 copy-start
  1.6 1.2 %copy-done = bf16[2,32,8192]{2,1,0:T(8,128)(2,1)S(1)} copy-done((bf16[2,32,8192]{2,1,0:T(8,128)(2,1)S(1)}, bf16[2,32,8192]{2,1,0:T(8,128)(2,1)}, u32[]{:S(2)}) %copy-start) | copy-done | bytes 1048600
  2.8 69.0 %shard_map.41 = (f32[2,32,8192]{2,1,0:T(8,128)S(1)}, f32[32,512]{1,0:T(8,128)S(1)}) custom-call(bf16[2,32,8192]{2,1,0:T(8,128)(2,1)S(1)} %copy-done, s32[512,32]{1,0:T(8,128)S(1)} %copy.4.omega_ref), custom_call_target="tpu_custom_call" | custom-call | flops 6000000000 | bytes 8388608 | tf_op jit(solution)/shard_map/pallas_call | solution.py:306
  71.8 1.3 %copy.7 = f32[2,32,8192]{2,1,0:T(8,128)} copy(f32[2,32,8192]{2,1,0:T(8,128)S(1)} %get-tuple-element.4) | data formatting | bytes 4194304
  73.2 0.6 copy.8
Async XLA Ops:
  1.6 1.2 %copy-start = (bf16[2,32,8192]{2,1,0:T(8,128)(2,1)S(1)}, bf16[2,32,8192]{2,1,0:T(8,128)(2,1)}, u32[]{:S(2)}) copy-start(bf16[2,32,8192]{2,1,0:T(8,128)(2,1)} %x_ref.1) | copy-start | bytes 3145732

commit v2 on v1

--- a/solution.py
+++ b/solution.py
@@ -10,7 +10,7 @@
 
 J = 16
 TEAM = 4
-CHUNKS = 4
+CHUNKS = 8
 HIGH = lax.Precision.HIGHEST
 NT = (((1,), (1,)), ((), ()))
 
@@ -42,9 +42,10 @@
 
 
 def kernel(count, x_ref, omega_ref, basis_ref, coupled_ref, halo, weights, sk, own, corr, gram_acc,
-           msg, rbuf, kred, kfin, p1s, p1r, dns, dnr, fws, fwr, srs, srr, m1s, m1r, m2s, m2r):
+           pack, gbuf, msg, rbuf, kred, kfin, xs, p1s, p1r, dns, dnr, fws, fwr, srs, srr, m0s, m0r, m1s, m1r,
+           m2s, m2r):
     per, inputs, width = x_ref.shape
-    rank = omega_ref.shape[1]
+    rank = omega_ref.shape[0]
     quarter = width // TEAM
     piece = quarter // CHUNKS
     level_lags = per * TEAM
@@ -105,16 +106,21 @@
         return remote(own.at[mate, k], own.at[mate, k], srs.at[k, s], srr.at[k, mate],
                       level * TEAM + mate)
 
+    def keep(k):
+        return pltpu.make_async_copy(x_ref.at[:, :, columns(place, k)],
+                                     halo.at[k, pl.ds(per * place, per)], xs.at[k])
+
     for k in range(CHUNKS):
         for s in (2, 3, 1):
             spread(k, s).start()
 
-    @pl.when(level > 0)
-    def _():
-        down(0, 0).start()
+        @pl.when(level > 0)
+        def _():
+            down(k, 0).start()
+
+        keep(k).start()
 
     for k in range(CHUNKS):
-        halo[k, pl.ds(per * place, per)] = x_ref[:, :, columns(place, k)]
         halo[k, lags - 1] = jnp.zeros((inputs, piece), jnp.bfloat16)
 
     @pl.when(level >= levels - 2)
@@ -130,13 +136,12 @@
                 (level_lags, inputs, piece), jnp.bfloat16)
 
     def own_down(k):
-        for s in range(TEAM):
-            if s:
-                spread_in(k, s).wait_recv()
-            if s or k:
-                @pl.when(level > 0)
-                def _():
-                    down(k, s).start()
+        for s in (1, 2, 3):
+            spread_in(k, s).wait_recv()
+
+            @pl.when(level > 0)
+            def _():
+                down(k, s).start()
 
     def pass_on(k):
         @pl.when(level < levels - 1)
@@ -149,6 +154,8 @@
                 forward(k).start()
 
     def compute(k):
+        keep(k).wait()
+
         @pl.when(level < levels - 2)
         def _():
             forward(k).wait_recv()
@@ -159,24 +166,42 @@
         for s in (2, 3, 1):
             give_back(k, s).start()
         own[place, k] = sk[k, pl.ds(per * place, per)]
+        wide = jnp.concatenate([sketch[i * rank : (i + 1) * rank] for i in range(level_lags)], axis=1)
+        local = lax.dot_general(wide, wide, NT, precision=HIGH, preferred_element_type=jnp.float32)
+        gram_acc[:, :rank] = local if k == 0 else gram_acc[:, :rank] + local
+        if k == CHUNKS - 1:
+            share_gram()
         parts = split3(sketch)
         product = sum(
             lax.dot_general(part, window, NT, preferred_element_type=jnp.float32)
             for part in reversed(parts)
         )
         corr[...] = product if k == 0 else corr[...] + product
-        wide = jnp.concatenate([sketch[i * rank : (i + 1) * rank] for i in range(level_lags)], axis=1)
-        local = lax.dot_general(wide, wide, NT, precision=HIGH, preferred_element_type=jnp.float32)
-        gram_acc[:, :rank] = local if k == 0 else gram_acc[:, :rank] + local
+
+    def gram_to(step):
+        other = lax.rem(me + step, count)
+        return remote(pack, gbuf.at[me], m0s.at[step], m0r.at[me], other)
+
+    def gram_in(step):
+        other = lax.rem(me + step, count)
+        return remote(pack, gbuf.at[other], m0s.at[step], m0r.at[other], other)
+
+    def share_gram():
+        packed = gram_acc[0:8, :]
+        for b in range(1, rank // 8):
+            packed = packed + pltpu.roll(gram_acc[8 * b : 8 * b + 8, :], b * rank, 1)
+        pack[...] = packed
+
+        @pl.loop(1, count)
+        def _(step):
+            gram_to(step).start()
+
+        gbuf[me] = packed
 
     own_down(0)
     own_down(1)
     gram_acc[...] = jnp.zeros_like(gram_acc)
-    probes = omega_ref[...].astype(jnp.float32) * 0.25
-    identity = jnp.where(
-        lax.broadcasted_iota(jnp.int32, (rank, rank), 0)
-        == lax.broadcasted_iota(jnp.int32, (rank, rank), 1), 1.0, 0.0)
-    turned = lax.dot_general(identity, probes, NT, preferred_element_type=jnp.float32)
+    turned = omega_ref[...].astype(jnp.float32) * 0.25
     band = jnp.concatenate(
         [turned, jnp.zeros((rank, weights.shape[1] - turned.shape[1]), jnp.float32)], axis=1)
     for i in range(level_lags):
@@ -197,18 +222,14 @@
     for i in range(1, level_lags):
         turned_back = pltpu.roll(corr[i * rank : (i + 1) * rank, :], lags * inputs - i * inputs, 1)
         folded = folded + turned_back[:, : J * inputs]
-    packed = gram_acc[0:8, :]
-    for b in range(1, rank // 8):
-        packed = packed + pltpu.roll(gram_acc[8 * b : 8 * b + 8, :], b * rank, 1)
     tiles_across = J * inputs // 128
     tiles = (rank // 8) * tiles_across
     for d in range(count):
-        msg[d, 0] = packed
         if d < tiles:
             a, b = divmod(d, tiles_across)
-            msg[d, 1] = folded[8 * a : 8 * a + 8, 128 * b : 128 * b + 128]
+            msg[d] = folded[8 * a : 8 * a + 8, 128 * b : 128 * b + 128]
         else:
-            msg[d, 1] = jnp.zeros((8, 128), jnp.float32)
+            msg[d] = jnp.zeros((8, 128), jnp.float32)
 
     def partial(step):
         other = lax.rem(me + step, count)
@@ -234,13 +255,19 @@
 
     @pl.loop(1, count)
     def _(step):
+        gram_in(step).wait_recv()
+
+    @pl.loop(1, count)
+    def _(step):
         partial_in(step).wait_recv()
 
-    total = rbuf[0]
+    product = rbuf[0]
+    total = gbuf[0]
     for d in range(1, count):
-        total = total + rbuf[d]
-    kred[...] = total[1]
-    kfin[me] = total[1]
+        product = product + rbuf[d]
+        total = total + gbuf[d]
+    kred[...] = product
+    kfin[me] = product
 
     @pl.loop(1, count)
     def _(step):
@@ -249,7 +276,7 @@
     lanes = lax.broadcasted_iota(jnp.int32, (8, 128), 1)
     blocks = []
     for b in range(rank // 8):
-        block = total[0] if b == 0 else pltpu.roll(total[0], 128 - b * rank, 1)
+        block = total if b == 0 else pltpu.roll(total, 128 - b * rank, 1)
         blocks.append(jnp.where(lanes < rank, block, 0.0))
     inverse = inverse_factor(jnp.concatenate(blocks, axis=0) * (1.0 / total_rows))
 
@@ -291,6 +318,7 @@
 
     @pl.loop(1, count)
     def _(step):
+        gram_to(step).wait_send()
         partial(step).wait_send()
         whole(step).wait_send()
 
@@ -309,7 +337,7 @@
             jax.ShapeDtypeStruct((per, rank, width), jnp.float32),
             jax.ShapeDtypeStruct((rank, J * inputs), jnp.float32),
         ),
-        in_specs=[vmem, vmem],
+        in_specs=[pl.BlockSpec(memory_space=pltpu.HBM), vmem],
         out_specs=(vmem, vmem),
         scratch_shapes=[
             pltpu.VMEM((CHUNKS, lags, inputs, piece), jnp.bfloat16),
@@ -318,19 +346,22 @@
             pltpu.VMEM((TEAM, CHUNKS, per, rank, piece), jnp.float32),
             pltpu.VMEM((level_lags * rank, lags * inputs), jnp.float32),
             pltpu.VMEM((rank, 128), jnp.float32),
-            pltpu.VMEM((count, 2, 8, 128), jnp.float32),
-            pltpu.VMEM((count, 2, 8, 128), jnp.float32),
             pltpu.VMEM((8, 128), jnp.float32),
             pltpu.VMEM((count, 8, 128), jnp.float32),
+            pltpu.VMEM((count, 8, 128), jnp.float32),
+            pltpu.VMEM((count, 8, 128), jnp.float32),
+            pltpu.VMEM((8, 128), jnp.float32),
+            pltpu.VMEM((count, 8, 128), jnp.float32),
+            dma((CHUNKS,)),
             dma((CHUNKS, TEAM)), dma((CHUNKS, TEAM)), dma((CHUNKS, TEAM)), dma((CHUNKS, TEAM)),
             dma((CHUNKS,)), dma((CHUNKS,)), dma((CHUNKS, TEAM)), dma((CHUNKS, TEAM)),
-            dma((count,)), dma((count,)), dma((count,)), dma((count,)),
+            dma((count,)), dma((count,)), dma((count,)), dma((count,)), dma((count,)), dma((count,)),
         ],
         compiler_params=pltpu.CompilerParams(
             collective_id=0, has_side_effects=True, vmem_limit_bytes=40 * 2**20
         ),
         cost_estimate=pl.CostEstimate(flops=6 * 10**9, bytes_accessed=8 * 2**20, transcendentals=0),
-    )(markov, omega)
+    )(markov, omega.T)
 
 
 def solution(mesh):

time: 74 us -> 70 us (0.946)
  Pallas kernels: 69 us -> 65.2 us
    pallas_call x1, Pallas kernels: 69 us -> 65.2 us  [per_device(): pl.pallas_call(functools.partial(kernel, count), out_shape=(jax.ShapeDtyp...]
    unnamed x5 -> x6, local copies, waits for them, and re-layouts: 4.13 us -> 4.01 us
where the time goes in v2:
time: 70 us; the launch traced here: 69.8 us
  Pallas kernels  65.2 us (93%)
  local copies, waits for them, and re-layouts  4.01 us (6%)
    pallas_call x1, Pallas kernels, per_device(): pl.pallas_call(functools.partial(kernel, count), out_shape=(jax.ShapeDtyp...  65.2 us
    unnamed x6, local copies, waits for them, and re-layouts  4.01 us

profile of v2, /device:TPU:0, one launch (start us, length us, event | category | flops | bytes accessed | tf_op | source)
XLA Modules:
  0.0 69.8 jit_solution(11184199655770733671)
XLA Ops:
  0.6 0.0 copy-start
  0.6 1.2 %copy-done = bf16[2,32,8192]{2,1,0:T(8,128)(2,1)S(1)} copy-done((bf16[2,32,8192]{2,1,0:T(8,128)(2,1)S(1)}, bf16[2,32,8192]{2,1,0:T(8,128)(2,1)}, u32[]{:S(2)}) %copy-start) | copy-done | bytes 1048600
  1.9 0.0 copy-start.1
  1.9 0.8 %copy-done.1 = s32[512,32]{0,1:T(8,128)S(1)} copy-done((s32[512,32]{0,1:T(8,128)S(1)}, s32[512,32]{0,1:T(8,128)}, u32[]{:S(2)}) %copy-start.1) | copy-done | bytes 65560
  2.7 65.2 %shard_map.41 = (f32[2,32,8192]{2,1,0:T(8,128)S(1)}, f32[32,512]{1,0:T(8,128)S(1)}) custom-call(bf16[2,32,8192]{2,1,0:T(8,128)(2,1)S(1)} %copy-done, s32[32,512]{1,0:T(8,128)S(1)} %bitcast.1), custom_call_target="tpu_custom_call" | custom-call | flops 6000000000 | bytes 8388608 | tf_op jit(solution)/shard_map/pallas_call | solution.py:334
  67.9 1.3 %copy.6 = f32[2,32,8192]{2,1,0:T(8,128)} copy(f32[2,32,8192]{2,1,0:T(8,128)S(1)} %get-tuple-element.4) | data formatting | bytes 4194304
  69.2 0.6 copy.7
Async XLA Ops:
  0.6 1.2 %copy-start = (bf16[2,32,8192]{2,1,0:T(8,128)(2,1)S(1)}, bf16[2,32,8192]{2,1,0:T(8,128)(2,1)}, u32[]{:S(2)}) copy-start(bf16[2,32,8192]{2,1,0:T(8,128)(2,1)} %x_ref.1) | copy-start | bytes 3145732
  1.9 0.8 %copy-start.1 = (s32[512,32]{0,1:T(8,128)S(1)}, s32[512,32]{0,1:T(8,128)}, u32[]{:S(2)}) copy-start(s32[512,32]{0,1:T(8,128)} %param.3) | copy-start | bytes 196612

commit v3 on v2

--- a/solution.py
+++ b/solution.py
@@ -41,8 +41,8 @@
     return pltpu.roll(work, 128 - size, 1)[:, :size]
 
 
-def kernel(count, x_ref, omega_ref, basis_ref, coupled_ref, halo, weights, sk, own, corr, gram_acc,
-           pack, gbuf, msg, rbuf, kred, kfin, xs, p1s, p1r, dns, dnr, fws, fwr, srs, srr, m0s, m0r, m1s, m1r,
+def kernel(count, x_ref, omega_ref, own, inverse_ref, summed_ref, halo, weights, sk, corr, gram_acc,
+           pack, gbuf, msg, rbuf, kred, kfin, xs, p1s, p1r, dns, dnr, fws, fwr, srs, srr, os, m0s, m0r, m1s, m1r,
            m2s, m2r):
     per, inputs, width = x_ref.shape
     rank = omega_ref.shape[0]
@@ -110,6 +110,9 @@
         return pltpu.make_async_copy(x_ref.at[:, :, columns(place, k)],
                                      halo.at[k, pl.ds(per * place, per)], xs.at[k])
 
+    def stay(k):
+        return pltpu.make_async_copy(sk.at[k, pl.ds(per * place, per)], own.at[place, k], os.at[k])
+
     for k in range(CHUNKS):
         for s in (2, 3, 1):
             spread(k, s).start()
@@ -165,7 +168,7 @@
         sk[k] = sketch.reshape(level_lags, rank, piece)
         for s in (2, 3, 1):
             give_back(k, s).start()
-        own[place, k] = sk[k, pl.ds(per * place, per)]
+        stay(k).start()
         wide = jnp.concatenate([sketch[i * rank : (i + 1) * rank] for i in range(level_lags)], axis=1)
         local = lax.dot_general(wide, wide, NT, precision=HIGH, preferred_element_type=jnp.float32)
         gram_acc[:, :rank] = local if k == 0 else gram_acc[:, :rank] + local
@@ -280,25 +283,20 @@
         blocks.append(jnp.where(lanes < rank, block, 0.0))
     inverse = inverse_factor(jnp.concatenate(blocks, axis=0) * (1.0 / total_rows))
 
+    inverse_ref[...] = inverse
+
+    @pl.loop(1, count)
+    def _(step):
+        whole_in(step).wait_recv()
+
+    summed_ref[...] = jnp.concatenate(
+        [jnp.concatenate([kfin[a * tiles_across + b] for b in range(tiles_across)], axis=1)
+         for a in range(rank // 8)], axis=0)
+
     for k in range(CHUNKS):
         for s in range(1, TEAM):
             give_back_in(k, s).wait_recv()
-    for q in range(TEAM):
-        for k in range(CHUNKS):
-            for g in range(per):
-                basis_ref[g, :, q * quarter + k * piece : q * quarter + (k + 1) * piece] = jnp.dot(
-                    inverse, own[q, k, g], precision=HIGH, preferred_element_type=jnp.float32)
-
-    @pl.loop(1, count)
-    def _(step):
-        whole_in(step).wait_recv()
-
-    summed = jnp.concatenate(
-        [jnp.concatenate([kfin[a * tiles_across + b] for b in range(tiles_across)], axis=1)
-         for a in range(rank // 8)], axis=0)
-    coupled_ref[...] = jnp.dot(
-        inverse, summed, precision=HIGH, preferred_element_type=jnp.float32
-    ) * (1.0 / math.sqrt(total_rows))
+        stay(k).wait()
 
     for k in range(CHUNKS):
         for s in range(1, TEAM):
@@ -321,6 +319,22 @@
         gram_to(step).wait_send()
         partial(step).wait_send()
         whole(step).wait_send()
+
+
+def whiten_kernel(total_rows, inverse_ref, summed_ref, own_ref, basis_ref, coupled_ref):
+    _, chunks, per, _, piece = own_ref.shape
+    inverse = inverse_ref[...]
+
+    @pl.when(pl.program_id(0) == 0)
+    def _():
+        coupled_ref[...] = jnp.dot(
+            inverse, summed_ref[...], precision=HIGH, preferred_element_type=jnp.float32
+        ) * (1.0 / math.sqrt(total_rows))
+
+    for k in range(chunks):
+        for g in range(per):
+            basis_ref[g, :, k * piece : (k + 1) * piece] = jnp.dot(
+                inverse, own_ref[0, k, g], precision=HIGH, preferred_element_type=jnp.float32)
 
 
 def per_device(count, markov, omega):
@@ -331,19 +345,19 @@
     lags = level_lags + J
     dma = pltpu.SemaphoreType.DMA
     vmem = pl.BlockSpec(memory_space=pltpu.VMEM)
-    return pl.pallas_call(
+    own, inverse, summed = pl.pallas_call(
         functools.partial(kernel, count),
         out_shape=(
-            jax.ShapeDtypeStruct((per, rank, width), jnp.float32),
+            jax.ShapeDtypeStruct((TEAM, CHUNKS, per, rank, piece), jnp.float32),
+            jax.ShapeDtypeStruct((rank, rank), jnp.float32),
             jax.ShapeDtypeStruct((rank, J * inputs), jnp.float32),
         ),
-        in_specs=[pl.BlockSpec(memory_space=pltpu.HBM), vmem],
-        out_specs=(vmem, vmem),
+        in_specs=[pl.BlockSpec(memory_space=pl.ANY), vmem],
+        out_specs=(pl.BlockSpec(memory_space=pl.ANY), vmem, vmem),
         scratch_shapes=[
             pltpu.VMEM((CHUNKS, lags, inputs, piece), jnp.bfloat16),
             pltpu.VMEM((level_lags * rank, lags * inputs), jnp.bfloat16),
             pltpu.VMEM((CHUNKS, level_lags, rank, piece), jnp.float32),
-            pltpu.VMEM((TEAM, CHUNKS, per, rank, piece), jnp.float32),
             pltpu.VMEM((level_lags * rank, lags * inputs), jnp.float32),
             pltpu.VMEM((rank, 128), jnp.float32),
             pltpu.VMEM((8, 128), jnp.float32),
@@ -354,14 +368,33 @@
             pltpu.VMEM((count, 8, 128), jnp.float32),
             dma((CHUNKS,)),
             dma((CHUNKS, TEAM)), dma((CHUNKS, TEAM)), dma((CHUNKS, TEAM)), dma((CHUNKS, TEAM)),
-            dma((CHUNKS,)), dma((CHUNKS,)), dma((CHUNKS, TEAM)), dma((CHUNKS, TEAM)),
+            dma((CHUNKS,)), dma((CHUNKS,)), dma((CHUNKS, TEAM)), dma((CHUNKS, TEAM)), dma((CHUNKS,)),
             dma((count,)), dma((count,)), dma((count,)), dma((count,)), dma((count,)), dma((count,)),
         ],
         compiler_params=pltpu.CompilerParams(
-            collective_id=0, has_side_effects=True, vmem_limit_bytes=40 * 2**20
+            collective_id=0, has_side_effects=True, vmem_limit_bytes=60 * 2**20
         ),
         cost_estimate=pl.CostEstimate(flops=6 * 10**9, bytes_accessed=8 * 2**20, transcendentals=0),
     )(markov, omega.T)
+    small = lambda shape: pl.BlockSpec(shape, lambda q: (0, 0))
+    return pl.pallas_call(
+        functools.partial(whiten_kernel, count * per * width),
+        grid=(TEAM,),
+        out_shape=(
+            jax.ShapeDtypeStruct((per, rank, width), jnp.float32),
+            jax.ShapeDtypeStruct((rank, J * inputs), jnp.float32),
+        ),
+        in_specs=[
+            small((rank, rank)),
+            small((rank, J * inputs)),
+            pl.BlockSpec((1, CHUNKS, per, rank, piece), lambda q: (q, 0, 0, 0, 0)),
+        ],
+        out_specs=(
+            pl.BlockSpec((per, rank, width // TEAM), lambda q: (0, 0, q)),
+            small((rank, J * inputs)),
+        ),
+        compiler_params=pltpu.CompilerParams(vmem_limit_bytes=60 * 2**20),
+    )(inverse, summed, own)
 
 
 def solution(mesh):

time: 70 us -> 71.9 us (1.027)
  Pallas kernels: 65.2 us -> 71 us
  local copies, waits for them, and re-layouts: 4.01 us -> 0 us
    pallas_call x0 -> x1, Pallas kernels: none -> 5.03 us  [per_device(): pl.pallas_call(functools.partial(whiten_kernel, count * per * width), gri...]
    unnamed x6 -> x0, local copies, waits for them, and re-layouts: 4.01 us -> none
    pallas_call x1, Pallas kernels: 65.2 us -> 66 us  [per_device(): pl.pallas_call(functools.partial(kernel, count), out_shape=(jax.ShapeDtyp...]
where the time goes in v3:
time: 71.9 us; the launch traced here: 71.7 us
  Pallas kernels  71 us (99%)
    pallas_call x1, Pallas kernels, per_device(): pl.pallas_call(functools.partial(kernel, count), out_shape=(jax.ShapeDtyp...  66 us
    pallas_call x1, Pallas kernels, per_device(): pl.pallas_call(functools.partial(whiten_kernel, count * per * width), gri...  5.03 us

profile of v3, /device:TPU:0, one launch (start us, length us, event | category | flops | bytes accessed | tf_op | source)
XLA Modules:
  0.0 71.7 jit_solution(7549040734245876876)
XLA Ops:
  0.6 66.0 %shard_map.41 = (f32[4,8,2,32,256]{4,3,2,1,0:T(8,128)}, f32[32,32]{1,0:T(8,128)}, f32[32,512]{1,0:T(8,128)}) custom-call(bf16[2,32,8192]{2,1,0:T(8,128)(2,1)} %x_ref.1, s32[32,512]{1,0:T(8,128)} %bitcast.1), custom_call_target="tpu_custom_call" | custom-call | flops 6000000000 | bytes 8388608 | tf_op jit(solution)/shard_map/pallas_call | solution.py:348
  66.6 5.0 %shard_map.42 = (f32[2,32,8192]{2,1,0:T(8,128)}, f32[32,512]{1,0:T(8,128)}) custom-call(f32[32,32]{1,0:T(8,128)} %get-tuple-element.5.inverse_ref, f32[32,512]{1,0:T(8,128)} %get-tuple-element.6.summed_ref, f32[4,8,2,32,256]{4,3,2,1,0:T(8,128)} %get-tuple-element.7.own_ref), custom_call_target="tpu_custom_call" | custom-call | tf_op jit(solution)/shard_map/pallas_call | solution.py:380

commit v4 on v2

--- a/solution.py
+++ b/solution.py
@@ -358,7 +358,7 @@
             dma((count,)), dma((count,)), dma((count,)), dma((count,)), dma((count,)), dma((count,)),
         ],
         compiler_params=pltpu.CompilerParams(
-            collective_id=0, has_side_effects=True, vmem_limit_bytes=40 * 2**20
+            collective_id=0, has_side_effects=True, vmem_limit_bytes=60 * 2**20
         ),
         cost_estimate=pl.CostEstimate(flops=6 * 10**9, bytes_accessed=8 * 2**20, transcendentals=0),
     )(markov, omega.T)

time: 70 us -> 72.2 us (1.031)
  Pallas kernels: 65.2 us -> 67.6 us
    pallas_call x1, Pallas kernels: 65.2 us -> 67.6 us  [per_device(): pl.pallas_call(functools.partial(kernel, count), out_shape=(jax.ShapeDtyp...]
    unnamed x6 -> x4, local copies, waits for them, and re-layouts: 4.01 us -> 3.73 us
where the time goes in v4:
time: 72.2 us; the launch traced here: 72 us
  Pallas kernels  67.6 us (94%)
  local copies, waits for them, and re-layouts  3.73 us (5%)
    pallas_call x1, Pallas kernels, per_device(): pl.pallas_call(functools.partial(kernel, count), out_shape=(jax.ShapeDtyp...  67.6 us
    unnamed x4, local copies, waits for them, and re-layouts  3.73 us

profile of v4, /device:TPU:0, one launch (start us, length us, event | category | flops | bytes accessed | tf_op | source)
XLA Modules:
  0.0 72.0 jit_solution(14371005886416453645)
XLA Ops:
  0.6 67.6 %shard_map.41 = (f32[2,32,8192]{2,1,0:T(8,128)}, f32[32,512]{1,0:T(8,128)}) custom-call(bf16[2,32,8192]{2,1,0:T(8,128)(2,1)} %x_ref.1, s32[32,512]{1,0:T(8,128)} %bitcast.1), custom_call_target="tpu_custom_call" | custom-call | flops 6000000000 | bytes 8388608 | tf_op jit(solution)/shard_map/pallas_call | solution.py:334
  68.2 0.0 copy-start
  68.2 3.1 %copy.6 = f32[2,32,8192]{2,1,0:T(8,128)} copy(f32[2,32,8192]{2,1,0:T(8,128)} %get-tuple-element.4) | data formatting | bytes 4194304
  71.3 0.0 copy-done
  71.3 0.6 copy.7
Async XLA Ops:
  68.2 3.1 %copy-start = (f32[32,512]{1,0:T(8,128)S(1)}, f32[32,512]{1,0:T(8,128)}, u32[]{:S(2)}) copy-start(f32[32,512]{1,0:T(8,128)} %get-tuple-element.5) | copy-start | bytes 196612

commit v5 on v2

--- a/solution.py
+++ b/solution.py
@@ -30,14 +30,11 @@
     work = gram + jnp.where(lanes == rows + size, 1.0, 0.0)
     for step in range(size):
         pivot_row = work[step : step + 1, :]
-        pivot = pivot_row[:, step : step + 1]
-        scale = lax.rsqrt(pivot)
-        scale = scale * (1.5 - 0.5 * pivot * scale * scale)
-        unit_row = pivot_row * scale
-        column = work[:, step : step + 1] * scale
-        work = jnp.where(
-            rows > step, work - column * unit_row, jnp.where(rows == step, unit_row, work)
-        )
+        unit_row = pivot_row / pivot_row[:, step : step + 1]
+        work = jnp.where(rows > step, work - work[:, step : step + 1] * unit_row, work)
+    pivots = jnp.sum(jnp.where(lanes == rows, work, 0.0), axis=1, keepdims=True)
+    scale = lax.rsqrt(pivots)
+    work = work * (scale * (1.5 - 0.5 * pivots * scale * scale))
     return pltpu.roll(work, 128 - size, 1)[:, :size]
 
 

time: 70 us -> 69.8 us (level)
  no operation moved by 1% of the time
where the time goes in v5:
time: 69.8 us; the launch traced here: 69.6 us
  Pallas kernels  65 us (93%)
  local copies, waits for them, and re-layouts  4.01 us (6%)
    pallas_call x1, Pallas kernels, per_device(): pl.pallas_call(functools.partial(kernel, count), out_shape=(jax.ShapeDtyp...  65 us
    unnamed x6, local copies, waits for them, and re-layouts  4.01 us

profile of v5, /device:TPU:0, one launch (start us, length us, event | category | flops | bytes accessed | tf_op | source)
XLA Modules:
  0.0 69.6 jit_solution(11991762237837829977)
XLA Ops:
  0.6 0.0 copy-start
  0.6 1.2 %copy-done = bf16[2,32,8192]{2,1,0:T(8,128)(2,1)S(1)} copy-done((bf16[2,32,8192]{2,1,0:T(8,128)(2,1)S(1)}, bf16[2,32,8192]{2,1,0:T(8,128)(2,1)}, u32[]{:S(2)}) %copy-start) | copy-done | bytes 1048600
  1.9 0.0 copy-start.1
  1.9 0.8 %copy-done.1 = s32[512,32]{0,1:T(8,128)S(1)} copy-done((s32[512,32]{0,1:T(8,128)S(1)}, s32[512,32]{0,1:T(8,128)}, u32[]{:S(2)}) %copy-start.1) | copy-done | bytes 65560
  2.7 65.0 %shard_map.41 = (f32[2,32,8192]{2,1,0:T(8,128)S(1)}, f32[32,512]{1,0:T(8,128)S(1)}) custom-call(bf16[2,32,8192]{2,1,0:T(8,128)(2,1)S(1)} %copy-done, s32[32,512]{1,0:T(8,128)S(1)} %bitcast.1), custom_call_target="tpu_custom_call" | custom-call | flops 6000000000 | bytes 8388608 | tf_op jit(solution)/shard_map/pallas_call | solution.py:331
  67.7 1.3 %copy.6 = f32[2,32,8192]{2,1,0:T(8,128)} copy(f32[2,32,8192]{2,1,0:T(8,128)S(1)} %get-tuple-element.4) | data formatting | bytes 4194304
  69.0 0.6 copy.7
Async XLA Ops:
  0.6 1.2 %copy-start = (bf16[2,32,8192]{2,1,0:T(8,128)(2,1)S(1)}, bf16[2,32,8192]{2,1,0:T(8,128)(2,1)}, u32[]{:S(2)}) copy-start(bf16[2,32,8192]{2,1,0:T(8,128)(2,1)} %x_ref.1) | copy-start | bytes 3145732
  1.9 0.8 %copy-start.1 = (s32[512,32]{0,1:T(8,128)S(1)}, s32[512,32]{0,1:T(8,128)}, u32[]{:S(2)}) copy-start(s32[512,32]{0,1:T(8,128)} %param.3) | copy-start | bytes 196612
